TPU v7x, 32 devices: a whole 2x2x4 slice. The times are simulated.
32 devices in a mesh: ens: 2 (over y), curve: 8 (over z, x), sub: 2 (over core).
Axes of the slice: x: 2, y: 2, z: 4, core: 2. Of those that a mesh axis runs over, the one named last changes fastest.
Arguments:
- conductivity: float32 [256, 4096], P(('ens', 'curve', 'sub')), parts along dimension 0, may hold values from 0.01 to 27
- neighbours: int32 [6, 256], P(None, ('ens', 'curve', 'sub')), parts along dimension 1, may hold values from -1 to 127, as said below
- live_count: int32 [32], P(('ens', 'curve', 'sub')), parts along dimension 0, may hold values from 0 to 8, as said below
Outputs:
- solution_field: float32 [3, 256, 4096], P(None, ('ens', 'curve', 'sub')), parts along dimension 1
- residual: float32 [3, 256, 4096], P(None, ('ens', 'curve', 'sub')), parts along dimension 1
There are 2 independent parts, one for each index of `ens`. A program takes and returns all parts, laid end to end along the dimension named above; each array names one. Nothing has to cross between parts.
Inputs may be any that keep to these rules, and one draw needn't show every extreme that they name: `live_count`: active bricks of a device fill its slots 0 to count - 1; some device has 8. Entries of empty slots are -1. The relation is symmetric across opposite sides. A -x or +x neighbour lies on the same device or on the device one before or one after along curve+sub, on the side named; all other neighbours lie on the same device. At most 4 bricks of a device have a +x neighbour on the next device, and some device reaches it.
All inputs are finite; a program needn't handle non-finite values.
Results may differ from a plain program's by a relative error of at most 0.00019.
Values sent between devices are 32-bit elements; how exact they have to be, the bound alone decides.
A program may use at most 64 MiB of HBM per device.

v0:
```python
import jax
import jax.numpy as jnp
from jax import lax
from jax.sharding import PartitionSpec as P

BRICK_EDGE_VOXELS = 16
ITERS = 4


def extended(value, sides, width):
    for axis, dim in sides:
        peers, length = (lax.axis_size(axis), value.shape[dim])
        up = [(i, (i + 1) % peers) for i in range(peers - 1)]
        down = [(j, i) for i, j in up]
        last = lax.slice_in_dim(value, length - width, length, axis=dim)
        leading = lax.slice_in_dim(value, 0, width, axis=dim)
        before = lax.ppermute(last, axis, up)
        after = lax.ppermute(leading, axis, down)
        value = jnp.concatenate([before, value, after], axis=dim)
    return value


def normal_axis(side):
    return (2, 2, 1, 1, 0, 0)[side]


def voxel_coords(brick):
    voxel = jnp.arange(brick**3, dtype=jnp.int32)
    return (voxel // (brick * brick), voxel // brick % brick, voxel % brick)


def x_table(side, brick):
    place = 0 if side % 2 == 0 else brick - 1
    coords = voxel_coords(brick)
    layer_index = coords[0] * brick + coords[1]
    column = jnp.arange(brick * brick, dtype=jnp.int32)
    hit = (coords[2][:, None] == place) & (layer_index[:, None] == column[None, :])
    return hit.astype(jnp.float32)


def face_layer(field, side, brick):
    lead = field.shape[:-1]
    place = 0 if side % 2 == 0 else brick - 1
    axis = normal_axis(side)
    if axis == 0:
        return lax.slice_in_dim(
            field, place * brick * brick, (place + 1) * brick * brick, axis=len(lead)
        )
    if axis == 1:
        rows = field.reshape(lead + (brick, brick * brick))
        part_rows = lax.slice_in_dim(rows, place * brick, (place + 1) * brick, axis=len(lead) + 1)
        return part_rows.reshape(lead + (brick * brick,))
    return jnp.dot(field, x_table(side, brick), precision=lax.Precision.HIGHEST)


def spread_face(face, side, brick):
    lead = face.shape[:-1]
    axis = normal_axis(side)
    if axis == 0:
        return jnp.tile(face, (1,) * len(lead) + (brick,))
    if axis == 1:
        rows = face.reshape(lead + (brick, brick))
        return jnp.tile(rows, (1,) * len(lead) + (1, brick)).reshape(lead + (brick**3,))
    return jnp.dot(face, x_table(side, brick).T, precision=lax.Precision.HIGHEST)


def inner_shift(field, side, brick):
    lead = field.shape[:-1]
    stride = (brick * brick, brick, 1)[normal_axis(side)]
    total = brick**3
    last = len(lead)
    blank = jnp.zeros(lead + (stride,), field.dtype)
    if side % 2 == 0:
        moved = jnp.concatenate(
            [blank, lax.slice_in_dim(field, 0, total - stride, axis=last)], last
        )
    else:
        moved = jnp.concatenate([lax.slice_in_dim(field, stride, total, axis=last), blank], last)
    return jnp.where(edge_mask(side, brick), 0.0, moved)


def edge_mask(side, brick):
    coords = voxel_coords(brick)
    target = 0 if side % 2 == 0 else brick - 1
    return coords[normal_axis(side)] == target


def beside_value(field, face, side, brick):
    return jnp.where(
        edge_mask(side, brick), spread_face(face, side, brick), inner_shift(field, side, brick)
    )


def build_plan(neighbours, slots):
    device_index = lax.axis_index(("curve", "sub"))
    valid = neighbours >= 0
    owner_device = jnp.where(valid, neighbours // slots, device_index)
    offset = owner_device - device_index
    local_slot = jnp.where(valid, neighbours % slots, 0)
    places = []
    senders = []
    for side in range(6):
        if side < 2:
            remote = valid[side] & (offset[side] != 0)
            places.append(jnp.where(remote, slots + local_slot[side], local_slot[side]))
        else:
            places.append(local_slot[side])
    return {"valid": valid, "places": places, "senders": senders}


def neighbour_faces(field, plan, keep_own):
    lower = face_layer(field, 0, BRICK_EDGE_VOXELS)
    upper = face_layer(field, 1, BRICK_EDGE_VOXELS)
    row_axis = lower.ndim - 2
    outer = extended(jnp.stack([lower, upper]), ((("curve", "sub"), 0),), 1)
    tables = [
        jnp.concatenate([upper, outer[0]], axis=row_axis),
        jnp.concatenate([lower, outer[3]], axis=row_axis),
    ]
    faces = []
    for side in range(6):
        if side < 2:
            picked = jnp.take(tables[side], plan["places"][side], axis=row_axis)
        else:
            picked = jnp.take(
                face_layer(field, side ^ 1, BRICK_EDGE_VOXELS), plan["places"][side], axis=row_axis
            )
        if keep_own:
            fill = (
                lower
                if side == 0
                else upper if side == 1 else face_layer(field, side, BRICK_EDGE_VOXELS)
            )
        else:
            fill = jnp.float32(0.0)
        faces.append(jnp.where(plan["valid"][side][:, None], picked, fill))
    return faces


def apply_operator(field, plan, weights, diagonal):
    faces = neighbour_faces(field, plan, False)
    result_field = diagonal * field
    for side in range(6):
        result_field = result_field - weights[side] * beside_value(
            field, faces[side], side, BRICK_EDGE_VOXELS
        )
    return result_field


def residual_product(residual, scaled):
    return lax.psum(jnp.sum(residual * scaled, axis=(1, 2)), ("curve", "sub"))


def local(conductivity, neighbours, live_count):
    slots = conductivity.shape[0]
    plan = build_plan(neighbours, slots)
    live = jnp.arange(slots, dtype=jnp.int32) < live_count[0]
    faces = neighbour_faces(conductivity, plan, True)
    weights = []
    for side in range(6):
        other = beside_value(conductivity, faces[side], side, BRICK_EDGE_VOXELS)
        weights.append(
            jnp.where(live[:, None], 2.0 * conductivity * other / (conductivity + other), 0.0)
        )
    total = weights[0]
    for side in range(1, 6):
        total = total + weights[side]
    diagonal = jnp.where(live[:, None], total, 1.0)
    rhs = jnp.stack([weights[1] - weights[0], weights[3] - weights[2], weights[5] - weights[4]])
    solution_field = jnp.zeros_like(rhs)
    residual = rhs
    scaled = residual / diagonal
    direction = scaled
    current = residual_product(residual, scaled)
    for step in range(ITERS):
        image = apply_operator(direction, plan, weights, diagonal)
        alpha = current / lax.psum(jnp.sum(direction * image, axis=(1, 2)), ("curve", "sub"))
        solution_field = solution_field + alpha[:, None, None] * direction
        residual = residual - alpha[:, None, None] * image
        if step + 1 < ITERS:
            scaled = residual / diagonal
            fresh = residual_product(residual, scaled)
            direction = scaled + (fresh / current)[:, None, None] * direction
            current = fresh
    return (solution_field, residual)


def solution(mesh):
    in_specs = (
        P(("ens", "curve", "sub"), None),
        P(None, ("ens", "curve", "sub")),
        P(("ens", "curve", "sub")),
    )
    out_specs = (P(None, ("ens", "curve", "sub"), None), P(None, ("ens", "curve", "sub"), None))
    return jax.shard_map(local, mesh=mesh, in_specs=in_specs, out_specs=out_specs, check_vma=False)
```

profile of v0, /device:TPU:0, one launch (start us, length us, event | category | flops | bytes accessed | tf_op | source)
XLA Modules:
  0.0 434.5 jit_solution(10621007083732256757)
XLA Ops:
  0.7 2.7 fusion.40
  3.4 2.4 collective-permute-start.1
  5.8 2.7 fusion.36
  8.5 1.5 collective-permute-start
  17.5 2.4 divide_select_fusion.4
  19.9 3.0 fusion.139
  23.0 2.4 fusion.103
  25.4 1.0 fusion.134
  26.5 2.4 fusion.114
  28.9 1.0 fusion.135
  31.4 5.9 %collective-permute-start.2 = (f32[1,3,8,256]{3,2,1,0:T(8,128)}, f32[1,3,8,256]{3,2,1,0:T(8,128)}, u32[]{:S(2)}, u32[]{:S(2)}) collective-permute-start(f32[1,3,8,256]{3,2,1,0:T(8,128)} %bitcast.28), channel_id=1, source_target_pairs={{0,1},{1,2},{2,3},{3,4},{4,5},{5,6},{6,7},{7,8},{8,9},{9,10},{10,1... | collective-permute-start | bytes 73736 | tf_op jit(solution)/shard_map/ppermute | solution.py:17
  39.8 1.2 tile.191
  41.0 3.2 tile.192
  44.3 1.0 reshape.256
  47.6 1.2 tile.194
  48.8 3.3 tile.195
  52.1 1.6 collective-permute-start.3
  62.0 4.2 fusion.31
  66.5 10.5 %multiply_reduce_fusion.6 = (f32[3]{0:T(128)}, f32[3]{0:T(128)}, f32[3,8,4096]{2,1,0:T(8,128)S(1)}) fusion(f32[3,8,4096]{2,1,0:T(8,128)S(1)} %broadcast_divide_fusion, f32[1,8,4096]{2,1,0:T(8,128)S(1)} %bitcast.258, f32[1,8,4096]{2,1,0:T(8,128)S(1)} %bitcast.252, f32[1,8,4096]{2,1,0:T(8,128)S(1)} %bitcast.264, f32[3,8,4096]{2,1,0:T(8,128)S(1)} %bitcast.273, ...), kind=kOutput, calls=%fused_computation.103 | convolution fusion | flops 306642944 | bytes 5776312 | tf_op jit(solution)/shard_map/dot_general | solution.py:64
  77.0 34.4 %all-reduce.30 = (f32[3]{0:T(128)S(1)}, f32[3]{0:T(128)S(1)}) all-reduce(f32[3]{0:T(128)} %get-tuple-element.6, f32[3]{0:T(128)} %get-tuple-element.4), channel_id=1, replica_groups=mesh['ens'=2,'curve'=8,'sub'=2] {'curve','sub'}, use_global_device_ids=true, to_apply=%region_1.4 | all-reduce | flops 6 | bytes 48 | tf_op jit(solution)/shard_map/psum | solution.py:151
  111.6 29.9 %psum.58 = f32[3]{0:T(128)S(1)} all-reduce(f32[3]{0:T(128)S(1)} %get-tuple-element.14), channel_id=1, replica_groups=mesh['ens'=2,'curve'=8,'sub'=2] {'curve','sub'}, use_global_device_ids=true, to_apply=%region_5.10 | all-reduce | flops 3 | bytes 24 | tf_op jit(solution)/shard_map/psum | solution.py:151
  141.7 3.1 fusion.111
  144.8 2.4 fusion.100
  147.2 1.0 fusion.129
  148.2 1.0 fusion.130
  149.3 0.9 fusion.132
  150.2 1.3 collective-permute-start.5
  151.5 3.6 collective-permute-start.4
  161.4 1.2 tile.201
  162.6 3.2 tile.202
  167.4 1.2 tile.204
  168.6 3.3 tile.205
  175.0 1.4 bitcast_select_fusion.16
  178.8 4.2 fusion.23
  183.2 10.4 %multiply_reduce_fusion.4 = (f32[3]{0:T(128)}, f32[3,8,4096]{2,1,0:T(8,128)S(1)}) fusion(f32[3,8,4096]{2,1,0:T(8,128)S(1)} %multiply_add_fusion.3, f32[3,8,4096]{2,1,0:T(8,128)S(1)} %bitcast.276, f32[3,8,3840]{2,1,0:T(8,128)S(1)} %copy-done.28, pred[4096]{0:T(1024)(128)(4,1)} %copy-done.75, f32[8,4096]{1,0:T(8,128)S(1)} %copy-done.45, ...), kind=kOutput, calls=%fused_computation.99 | convolution fusion | flops 306249728 | bytes 5383084 | tf_op jit(solution)/shard_map/dot_general | solution.py:64
  193.6 30.3 %psum.59 = f32[3]{0:T(128)S(1)} all-reduce(f32[3]{0:T(128)} %get-tuple-element.111), channel_id=1, replica_groups=mesh['ens'=2,'curve'=8,'sub'=2] {'curve','sub'}, use_global_device_ids=true, to_apply=%region_7.12 | all-reduce | flops 3 | bytes 24 | tf_op jit(solution)/shard_map/psum | solution.py:177
  224.7 29.5 %psum.60 = f32[3]{0:T(128)S(1)} all-reduce(f32[3]{0:T(128)S(1)} %get-tuple-element.12), channel_id=1, replica_groups=mesh['ens'=2,'curve'=8,'sub'=2] {'curve','sub'}, use_global_device_ids=true, to_apply=%region_9.14 | all-reduce | flops 3 | bytes 24 | tf_op jit(solution)/shard_map/psum | solution.py:151
  254.9 3.1 fusion.108
  258.0 2.4 fusion.97
  262.4 1.3 collective-permute-start.7
  263.7 3.6 collective-permute-start.6
  271.2 1.9 tile.211
  273.2 3.8 tile.212
  277.1 1.9 tile.214
  279.0 3.8 tile.215
  285.6 1.4 bitcast_select_fusion.10
  289.3 4.2 fusion.15
  294.4 4.8 %multiply_reduce_fusion.2 = (f32[3]{0:T(128)S(1)}, f32[3,8,4096]{2,1,0:T(8,128)}) fusion(f32[3,8,4096]{2,1,0:T(8,128)S(1)} %multiply_add_fusion.2, f32[3,8,4096]{2,1,0:T(8,128)S(1)} %bitcast.277, f32[3,8,3840]{2,1,0:T(8,128)S(1)} %copy-done.30, pred[4096]{0:T(1024)(128)(4,1)S(1)} %copy-done.76, f32[8,4096]{1,0:T(8,128)} %copy-done.43, ...), kind=kOutput, calls=%fused_computation.95 | convolution fusion | flops 306249728 | bytes 5383084 | tf_op jit(solution)/shard_map/dot_general | solution.py:64
  299.2 30.0 %psum.61 = f32[3]{0:T(128)S(1)} all-reduce(f32[3]{0:T(128)S(1)} %get-tuple-element.113), channel_id=1, replica_groups=mesh['ens'=2,'curve'=8,'sub'=2] {'curve','sub'}, use_global_device_ids=true, to_apply=%region_11.16 | all-reduce | flops 3 | bytes 24 | tf_op jit(solution)/shard_map/psum | solution.py:177
  329.2 1.2 multiply_reduce_fusion.1
  330.4 29.7 %psum.62 = f32[3]{0:T(128)S(1)} all-reduce(f32[3]{0:T(128)S(1)} %get-tuple-element.10), channel_id=1, replica_groups=mesh['ens'=2,'curve'=8,'sub'=2] {'curve','sub'}, use_global_device_ids=true, to_apply=%region_13.18 | all-reduce | flops 3 | bytes 24 | tf_op jit(solution)/shard_map/psum | solution.py:151
  360.2 2.4 fusion.94
  362.6 2.4 fusion.105
  365.9 1.0 fusion.120
  367.8 2.4 collective-permute-start.8
  370.2 1.3 collective-permute-start.9
  375.2 1.9 tile.221
  377.1 3.8 tile.222
  381.0 1.9 tile.224
  383.0 3.8 tile.225
  390.6 4.1 fusion.7
  394.9 5.9 %multiply_reduce_fusion = (f32[3]{0:T(128)}, f32[3,8,4096]{2,1,0:T(8,128)}) fusion(f32[3,8,4096]{2,1,0:T(8,128)S(1)} %multiply_add_fusion.1, f32[3,8,4096]{2,1,0:T(8,128)S(1)} %bitcast.271, f32[3,8,3840]{2,1,0:T(8,128)} %get-tuple-element.41, pred[4096]{0:T(1024)(128)(4,1)S(1)} %copy-done.77, f32[8,4096]{1,0:T(8,128)} %copy-done.43, ...), kind=kOutput, calls=%fused_computation.91 | convolution fusion | flops 306249728 | bytes 5383084 | tf_op jit(solution)/shard_map/dot_general | solution.py:64
  400.8 30.7 %psum.63 = f32[3]{0:T(128)S(1)} all-reduce(f32[3]{0:T(128)} %get-tuple-element.115), channel_id=1, replica_groups=mesh['ens'=2,'curve'=8,'sub'=2] {'curve','sub'}, use_global_device_ids=true, to_apply=%region_15.20 | all-reduce | flops 3 | bytes 24 | tf_op jit(solution)/shard_map/psum | solution.py:177
  432.2 2.1 multiply_subtract_fusion
  (440 shorter events, 58.1 us)
Async XLA Ops:
  0.6 9.7 %copy-start.78 = (s32[6,8]{1,0:T(8,128)S(1)}, s32[6,8]{1,0:T(8,128)}, u32[]{:S(2)}) copy-start(s32[6,8]{1,0:T(8,128)} %param.12) | copy-start | bytes 580
  0.7 25.8 %copy-start.79 = (s32[4096]{0:T(1024)}, s32[4096]{0:T(1024)S(1)}, u32[]{:S(2)}) copy-start(s32[4096]{0:T(1024)S(1)} %fusion.70) | copy-start | bytes 49156
  0.7 22.3 %copy-start.100 = (pred[4096]{0:T(1024)(128)(4,1)}, pred[4096]{0:T(1024)(128)(4,1)S(1)}, u32[]{:S(2)}) copy-start(pred[4096]{0:T(1024)(128)(4,1)S(1)} %fusion.74) | copy-start | bytes 12292
  3.4 12.9 %collective-permute-start.1 = (f32[1,8,256]{2,1,0:T(8,128)S(1)}, f32[1,8,256]{2,1,0:T(8,128)S(1)}, u32[]{:S(2)}, u32[]{:S(2)}) collective-permute-start(f32[1,8,256]{2,1,0:T(8,128)S(1)} %bitcast.280), channel_id=1, source_target_pairs={{0,1},{1,2},{2,3},{3,4},{4,5},{5,6},{6,7},{7,8},{8,9},{9,10},{10,1... | collective-permute-start | bytes 24584 | tf_op jit(solution)/shard_map/ppermute | solution.py:17
  5.8 20.7 %copy-start.104 = (pred[4096]{0:T(1024)(128)(4,1)}, pred[4096]{0:T(1024)(128)(4,1)S(1)}, u32[]{:S(2)}) copy-start(pred[4096]{0:T(1024)(128)(4,1)S(1)} %fusion.73) | copy-start | bytes 12292
  8.5 8.4 %collective-permute-start = (f32[1,8,256]{2,1,0:T(8,128)S(1)}, f32[1,8,256]{2,1,0:T(8,128)S(1)}, u32[]{:S(2)}, u32[]{:S(2)}) collective-permute-start(f32[1,8,256]{2,1,0:T(8,128)S(1)} %bitcast.282), channel_id=1, source_target_pairs={{1,0},{2,1},{3,2},{4,3},{5,4},{6,5},{7,6},{8,7},{9,8},{10,9},{11,1... | collective-permute-start | bytes 24584 | tf_op jit(solution)/shard_map/ppermute | solution.py:18
  10.5 28.4 %copy-start.58 = (pred[8]{0:T(512)(128)(4,1)}, pred[8]{0:T(512)(128)(4,1)S(1)}, u32[]{:S(2)}) copy-start(pred[8]{0:T(512)(128)(4,1)S(1)} %get-tuple-element.95) | copy-start | bytes 28
  12.3 26.0 %copy-start.99 = (s32[1024]{0:T(1024)}, s32[1024]{0:T(1024)S(1)}, u32[]{:S(2)}) copy-start(s32[1024]{0:T(1024)S(1)} %pad_clamp_fusion.2) | copy-start | bytes 12292
  22.9 14.4 %copy-start.12 = (f32[8,4096]{1,0:T(8,128)}, f32[8,4096]{1,0:T(8,128)S(1)}, u32[]{:S(2)}) copy-start(f32[8,4096]{1,0:T(8,128)S(1)} %get-tuple-element.74) | copy-start | bytes 393220
  22.9 14.4 %copy-start = (f32[8,4096]{1,0:T(8,128)}, f32[8,4096]{1,0:T(8,128)S(1)}, u32[]{:S(2)}) copy-start(f32[8,4096]{1,0:T(8,128)S(1)} %get-tuple-element.75) | copy-start | bytes 393220
  31.4 26.0 %collective-permute-start.2 = (f32[1,3,8,256]{3,2,1,0:T(8,128)}, f32[1,3,8,256]{3,2,1,0:T(8,128)}, u32[]{:S(2)}, u32[]{:S(2)}) collective-permute-start(f32[1,3,8,256]{3,2,1,0:T(8,128)} %bitcast.28), channel_id=1, source_target_pairs={{0,1},{1,2},{2,3},{3,4},{4,5},{5,6},{6,7},{7,8},{8,9},{9,10},{10,1... | collective-permute-start | bytes 73736 | tf_op jit(solution)/shard_map/ppermute | solution.py:17
  52.0 14.3 %copy-start.5 = (f32[8,4096]{1,0:T(8,128)S(1)}, f32[8,4096]{1,0:T(8,128)}, u32[]{:S(2)}) copy-start(f32[8,4096]{1,0:T(8,128)} %copy-done.4) | copy-start | bytes 393220
  52.1 14.3 %copy-start.8 = (f32[8,4096]{1,0:T(8,128)S(1)}, f32[8,4096]{1,0:T(8,128)}, u32[]{:S(2)}) copy-start(f32[8,4096]{1,0:T(8,128)} %copy-done.7) | copy-start | bytes 393220
  52.1 14.3 %copy-start.13 = (f32[8,4096]{1,0:T(8,128)S(1)}, f32[8,4096]{1,0:T(8,128)}, u32[]{:S(2)}) copy-start(f32[8,4096]{1,0:T(8,128)} %copy-done.12) | copy-start | bytes 393220
  52.1 14.3 %copy-start.15 = (f32[3,8,4096]{2,1,0:T(8,128)S(1)}, f32[3,8,4096]{2,1,0:T(8,128)}, u32[]{:S(2)}) copy-start(f32[3,8,4096]{2,1,0:T(8,128)} %tile.192) | copy-start | bytes 1179652
  52.1 14.3 %copy-start.16 = (f32[3,8,4096]{2,1,0:T(8,128)S(1)}, f32[3,8,4096]{2,1,0:T(8,128)}, u32[]{:S(2)}) copy-start(f32[3,8,4096]{2,1,0:T(8,128)} %tile.195) | copy-start | bytes 1179652
  52.1 14.3 %copy-start.19 = (f32[3,8,4095]{2,1,0:T(8,128)S(1)}, f32[3,8,4095]{2,1,0:T(8,128)}, u32[]{:S(2)}) copy-start(f32[3,8,4095]{2,1,0:T(8,128)} %get-tuple-element.64) | copy-start | bytes 1179364
  52.1 14.3 %copy-start.20 = (f32[3,8,4080]{2,1,0:T(8,128)S(1)}, f32[3,8,4080]{2,1,0:T(8,128)}, u32[]{:S(2)}) copy-start(f32[3,8,4080]{2,1,0:T(8,128)} %get-tuple-element.66) | copy-start | bytes 1175044
  52.1 14.3 %copy-start.21 = (f32[3,8,4080]{2,1,0:T(8,128)S(1)}, f32[3,8,4080]{2,1,0:T(8,128)}, u32[]{:S(2)}) copy-start(f32[3,8,4080]{2,1,0:T(8,128)} %get-tuple-element.67) | copy-start | bytes 1175044
  52.1 14.3 %copy-start.32 = (f32[8,4096]{1,0:T(8,128)S(1)}, f32[8,4096]{1,0:T(8,128)}, u32[]{:S(2)}) copy-start(f32[8,4096]{1,0:T(8,128)} %copy-done.31) | copy-start | bytes 393220
  52.1 14.3 %copy-start.37 = (f32[8,4096]{1,0:T(8,128)S(1)}, f32[8,4096]{1,0:T(8,128)}, u32[]{:S(2)}) copy-start(f32[8,4096]{1,0:T(8,128)} %copy-done.36) | copy-start | bytes 393220
  52.1 7.5 %collective-permute-start.3 = (f32[1,3,8,256]{3,2,1,0:T(8,128)}, f32[1,3,8,256]{3,2,1,0:T(8,128)S(1)}, u32[]{:S(2)}, u32[]{:S(2)}) collective-permute-start(f32[1,3,8,256]{3,2,1,0:T(8,128)} %bitcast.278), channel_id=1, source_target_pairs={{1,0},{2,1},{3,2},{4,3},{5,4},{6,5},{7,6},{8,7},{9,8},{10,9},{11,1... | collective-permute-start | bytes 73736 | tf_op jit(solution)/shard_map/ppermute | solution.py:18
  66.5 44.9 %copy-start.1 = (f32[8,4096]{1,0:T(8,128)S(1)}, f32[8,4096]{1,0:T(8,128)}, u32[]{:S(2)}) copy-start(f32[8,4096]{1,0:T(8,128)} %copy-done) | copy-start | bytes 393220
  77.0 67.8 %copy-start.81 = (s32[4096]{0:T(1024)S(1)}, s32[4096]{0:T(1024)}, u32[]{:S(2)}) copy-start(s32[4096]{0:T(1024)} %copy-done.79) | copy-start | bytes 49156
  77.0 67.8 %copy-start.101 = (pred[4096]{0:T(1024)(128)(4,1)S(1)}, pred[4096]{0:T(1024)(128)(4,1)}, u32[]{:S(2)}) copy-start(pred[4096]{0:T(1024)(128)(4,1)} %copy-done.100) | copy-start | bytes 12292
  111.4 35.8 %copy-start.107 = (f32[3]{0:T(128)}, f32[3]{0:T(128)S(1)}, u32[]{:S(2)}) copy-start(f32[3]{0:T(128)S(1)} %div.429) | copy-start | bytes 40
  111.6 36.6 %copy-start.10 = (f32[3,8,4096]{2,1,0:T(8,128)}, f32[3,8,4096]{2,1,0:T(8,128)S(1)}, u32[]{:S(2)}) copy-start(f32[3,8,4096]{2,1,0:T(8,128)S(1)} %get-tuple-element.15) | copy-start | bytes 1179652
  147.2 9.9 %copy-start.51 = (pred[8]{0:T(512)(128)(4,1)S(1)}, pred[8]{0:T(512)(128)(4,1)}, u32[]{:S(2)}) copy-start(pred[8]{0:T(512)(128)(4,1)} %copy-done.50) | copy-start | bytes 28
  147.2 9.9 %copy-start.63 = (pred[8]{0:T(512)(128)(4,1)S(1)}, pred[8]{0:T(512)(128)(4,1)}, u32[]{:S(2)}) copy-start(pred[8]{0:T(512)(128)(4,1)} %copy-done.62) | copy-start | bytes 28
  148.2 10.3 %copy-start.55 = (pred[8]{0:T(512)(128)(4,1)S(1)}, pred[8]{0:T(512)(128)(4,1)}, u32[]{:S(2)}) copy-start(pred[8]{0:T(512)(128)(4,1)} %copy-done.54) | copy-start | bytes 28
  150.2 23.4 %collective-permute-start.5 = (f32[1,3,8,256]{3,2,1,0:T(8,128)}, f32[1,3,8,256]{3,2,1,0:T(8,128)}, u32[]{:S(2)}, u32[]{:S(2)}) collective-permute-start(f32[1,3,8,256]{3,2,1,0:T(8,128)} %bitcast.48), channel_id=1, source_target_pairs={{1,0},{2,1},{3,2},{4,3},{5,4},{6,5},{7,6},{8,7},{9,8},{10,9},{11,1... | collective-permute-start | bytes 73736 | tf_op jit(solution)/shard_map/ppermute | solution.py:18
  151.5 24.9 %collective-permute-start.4 = (f32[1,3,8,256]{3,2,1,0:T(8,128)}, f32[1,3,8,256]{3,2,1,0:T(8,128)}, u32[]{:S(2)}, u32[]{:S(2)}) collective-permute-start(f32[1,3,8,256]{3,2,1,0:T(8,128)} %bitcast.45), channel_id=1, source_target_pairs={{0,1},{1,2},{2,3},{3,4},{4,5},{5,6},{6,7},{7,8},{8,9},{9,10},{10,1... | collective-permute-start | bytes 73736 | tf_op jit(solution)/shard_map/ppermute | solution.py:17
  171.8 11.2 %copy-start.17 = (f32[3,8,4096]{2,1,0:T(8,128)S(1)}, f32[3,8,4096]{2,1,0:T(8,128)}, u32[]{:S(2)}) copy-start(f32[3,8,4096]{2,1,0:T(8,128)} %tile.202) | copy-start | bytes 1179652
  171.8 11.2 %copy-start.18 = (f32[3,8,4096]{2,1,0:T(8,128)S(1)}, f32[3,8,4096]{2,1,0:T(8,128)}, u32[]{:S(2)}) copy-start(f32[3,8,4096]{2,1,0:T(8,128)} %tile.205) | copy-start | bytes 1179652
  171.8 11.3 %copy-start.22 = (f32[3,8,4095]{2,1,0:T(8,128)S(1)}, f32[3,8,4095]{2,1,0:T(8,128)}, u32[]{:S(2)}) copy-start(f32[3,8,4095]{2,1,0:T(8,128)} %get-tuple-element.54) | copy-start | bytes 1179364
  171.8 11.3 %copy-start.23 = (f32[3,8,4080]{2,1,0:T(8,128)S(1)}, f32[3,8,4080]{2,1,0:T(8,128)}, u32[]{:S(2)}) copy-start(f32[3,8,4080]{2,1,0:T(8,128)} %get-tuple-element.56) | copy-start | bytes 1175044
  171.8 11.3 %copy-start.24 = (f32[3,8,4080]{2,1,0:T(8,128)S(1)}, f32[3,8,4080]{2,1,0:T(8,128)}, u32[]{:S(2)}) copy-start(f32[3,8,4080]{2,1,0:T(8,128)} %get-tuple-element.57) | copy-start | bytes 1175044
  171.8 11.3 %copy-start.33 = (f32[8,4096]{1,0:T(8,128)S(1)}, f32[8,4096]{1,0:T(8,128)}, u32[]{:S(2)}) copy-start(f32[8,4096]{1,0:T(8,128)} %copy-done.31) | copy-start | bytes 393220
  171.8 11.3 %copy-start.38 = (f32[8,4096]{1,0:T(8,128)S(1)}, f32[8,4096]{1,0:T(8,128)}, u32[]{:S(2)}) copy-start(f32[8,4096]{1,0:T(8,128)} %copy-done.36) | copy-start | bytes 393220
  183.0 41.5 %copy-start.2 = (f32[8,4096]{1,0:T(8,128)S(1)}, f32[8,4096]{1,0:T(8,128)}, u32[]{:S(2)}) copy-start(f32[8,4096]{1,0:T(8,128)} %copy-done) | copy-start | bytes 393220
  183.0 41.5 %copy-start.11 = (f32[3,8,4096]{2,1,0:T(8,128)S(1)}, f32[3,8,4096]{2,1,0:T(8,128)}, u32[]{:S(2)}) copy-start(f32[3,8,4096]{2,1,0:T(8,128)} %copy-done.10) | copy-start | bytes 1179652
  193.6 64.4 %copy-start.83 = (s32[4096]{0:T(1024)S(1)}, s32[4096]{0:T(1024)}, u32[]{:S(2)}) copy-start(s32[4096]{0:T(1024)} %copy-done.79) | copy-start | bytes 49156
  193.6 64.4 %copy-start.102 = (pred[4096]{0:T(1024)(128)(4,1)S(1)}, pred[4096]{0:T(1024)(128)(4,1)}, u32[]{:S(2)}) copy-start(pred[4096]{0:T(1024)(128)(4,1)} %copy-done.100) | copy-start | bytes 12292
  224.5 36.0 %copy-start.108 = (f32[3]{0:T(128)}, f32[3]{0:T(128)S(1)}, u32[]{:S(2)}) copy-start(f32[3]{0:T(128)S(1)} %div.432) | copy-start | bytes 40
  262.4 21.6 %collective-permute-start.7 = (f32[1,3,8,256]{3,2,1,0:T(8,128)}, f32[1,3,8,256]{3,2,1,0:T(8,128)}, u32[]{:S(2)}, u32[]{:S(2)}) collective-permute-start(f32[1,3,8,256]{3,2,1,0:T(8,128)} %bitcast.61), channel_id=1, source_target_pairs={{1,0},{2,1},{3,2},{4,3},{5,4},{6,5},{7,6},{8,7},{9,8},{10,9},{11,1... | collective-permute-start | bytes 73736 | tf_op jit(solution)/shard_map/ppermute | solution.py:18
  263.7 23.2 %collective-permute-start.6 = (f32[1,3,8,256]{3,2,1,0:T(8,128)}, f32[1,3,8,256]{3,2,1,0:T(8,128)}, u32[]{:S(2)}, u32[]{:S(2)}) collective-permute-start(f32[1,3,8,256]{3,2,1,0:T(8,128)} %bitcast.58), channel_id=1, source_target_pairs={{0,1},{1,2},{2,3},{3,4},{4,5},{5,6},{6,7},{7,8},{8,9},{9,10},{10,1... | collective-permute-start | bytes 73736 | tf_op jit(solution)/shard_map/ppermute | solution.py:17
  282.8 11.5 %copy-start.34 = (f32[8,4096]{1,0:T(8,128)S(1)}, f32[8,4096]{1,0:T(8,128)}, u32[]{:S(2)}) copy-start(f32[8,4096]{1,0:T(8,128)} %copy-done.31) | copy-start | bytes 393220
  282.8 11.5 %copy-start.67 = (pred[4096]{0:T(1024)(128)(4,1)S(1)}, pred[4096]{0:T(1024)(128)(4,1)}, u32[]{:S(2)}) copy-start(pred[4096]{0:T(1024)(128)(4,1)} %copy-done.66) | copy-start | bytes 12292
  282.8 11.5 %copy-start.70 = (pred[4096]{0:T(1024)(128)(4,1)S(1)}, pred[4096]{0:T(1024)(128)(4,1)}, u32[]{:S(2)}) copy-start(pred[4096]{0:T(1024)(128)(4,1)} %copy-done.69) | copy-start | bytes 12292
  282.8 11.5 %copy-start.73 = (pred[4096]{0:T(1024)(128)(4,1)S(1)}, pred[4096]{0:T(1024)(128)(4,1)}, u32[]{:S(2)}) copy-start(pred[4096]{0:T(1024)(128)(4,1)} %copy-done.72) | copy-start | bytes 12292
  282.8 11.5 %copy-start.76 = (pred[4096]{0:T(1024)(128)(4,1)S(1)}, pred[4096]{0:T(1024)(128)(4,1)}, u32[]{:S(2)}) copy-start(pred[4096]{0:T(1024)(128)(4,1)} %copy-done.75) | copy-start | bytes 12292
  293.5 35.7 %copy-start.113 = (f32[3]{0:T(128)S(1)}, f32[3]{0:T(128)}, u32[]{:S(2)}) copy-start(f32[3]{0:T(128)} %copy-done.112) | copy-start | bytes 40
  294.4 65.8 %copy-start.84 = (s32[4096]{0:T(1024)S(1)}, s32[4096]{0:T(1024)}, u32[]{:S(2)}) copy-start(s32[4096]{0:T(1024)} %copy-done.79) | copy-start | bytes 49156
  294.4 65.8 %copy-start.103 = (pred[4096]{0:T(1024)(128)(4,1)S(1)}, pred[4096]{0:T(1024)(128)(4,1)}, u32[]{:S(2)}) copy-start(pred[4096]{0:T(1024)(128)(4,1)} %copy-done.100) | copy-start | bytes 12292
  299.2 63.5 %copy-start.105 = (pred[4096]{0:T(1024)(128)(4,1)S(1)}, pred[4096]{0:T(1024)(128)(4,1)}, u32[]{:S(2)}) copy-start(pred[4096]{0:T(1024)(128)(4,1)} %copy-done.104) | copy-start | bytes 12292
  329.2 35.9 %copy-start.109 = (f32[3]{0:T(128)}, f32[3]{0:T(128)S(1)}, u32[]{:S(2)}) copy-start(f32[3]{0:T(128)S(1)} %div.435) | copy-start | bytes 40
  365.0 9.7 %copy-start.53 = (pred[8]{0:T(512)(128)(4,1)S(1)}, pred[8]{0:T(512)(128)(4,1)}, u32[]{:S(2)}) copy-start(pred[8]{0:T(512)(128)(4,1)} %copy-done.50) | copy-start | bytes 28
  365.0 9.8 %copy-start.61 = (pred[8]{0:T(512)(128)(4,1)S(1)}, pred[8]{0:T(512)(128)(4,1)}, u32[]{:S(2)}) copy-start(pred[8]{0:T(512)(128)(4,1)} %copy-done.58) | copy-start | bytes 28
  365.0 9.8 %copy-start.65 = (pred[8]{0:T(512)(128)(4,1)S(1)}, pred[8]{0:T(512)(128)(4,1)}, u32[]{:S(2)}) copy-start(pred[8]{0:T(512)(128)(4,1)} %copy-done.62) | copy-start | bytes 28
  367.8 19.6 %collective-permute-start.8 = (f32[1,3,8,256]{3,2,1,0:T(8,128)}, f32[1,3,8,256]{3,2,1,0:T(8,128)}, u32[]{:S(2)}, u32[]{:S(2)}) collective-permute-start(f32[1,3,8,256]{3,2,1,0:T(8,128)} %bitcast.71), channel_id=1, source_target_pairs={{0,1},{1,2},{2,3},{3,4},{4,5},{5,6},{6,7},{7,8},{8,9},{9,10},{10,1... | collective-permute-start | bytes 73736 | tf_op jit(solution)/shard_map/ppermute | solution.py:17
  370.2 18.8 %collective-permute-start.9 = (f32[1,3,8,256]{3,2,1,0:T(8,128)}, f32[1,3,8,256]{3,2,1,0:T(8,128)}, u32[]{:S(2)}, u32[]{:S(2)}) collective-permute-start(f32[1,3,8,256]{3,2,1,0:T(8,128)} %bitcast.74), channel_id=1, source_target_pairs={{1,0},{2,1},{3,2},{4,3},{5,4},{6,5},{7,6},{8,7},{9,8},{10,9},{11,1... | collective-permute-start | bytes 73736 | tf_op jit(solution)/shard_map/ppermute | solution.py:18
  394.8 37.4 %copy-start.6 = (f32[8,4096]{1,0:T(8,128)S(1)}, f32[8,4096]{1,0:T(8,128)}, u32[]{:S(2)}) copy-start(f32[8,4096]{1,0:T(8,128)} %copy-done.4) | copy-start | bytes 393220
  394.8 37.4 %copy-start.9 = (f32[8,4096]{1,0:T(8,128)S(1)}, f32[8,4096]{1,0:T(8,128)}, u32[]{:S(2)}) copy-start(f32[8,4096]{1,0:T(8,128)} %copy-done.7) | copy-start | bytes 393220
  394.8 37.4 %copy-start.14 = (f32[8,4096]{1,0:T(8,128)S(1)}, f32[8,4096]{1,0:T(8,128)}, u32[]{:S(2)}) copy-start(f32[8,4096]{1,0:T(8,128)} %copy-done.12) | copy-start | bytes 393220
  (64 other events, 423.8 us)
where the time goes:
time: 440 us; the launch traced here: 435 us
  blocking collectives  214 us (49%)
  local copies, waits for them, and re-layouts  88.5 us (20%)
  matrix products  79.8 us (18%)
  starting transfers between devices  24.8 us (6%)
  other arithmetic  23 us (5%)
    psum x4, blocking collectives, residual_product(): return lax.psum(jnp.sum(residual * scaled, axis=(1, 2)), ('curve', 'sub'))  123 us
    psum x3, blocking collectives, local(): lax.psum(jnp.sum(direction * image, axis=(1, 2)), ('curve', 'sub'))  91 us
    dot_general x10, matrix products, spread_face(): jnp.dot(face, x_table(side, brick).T, precision=lax.Precision.HIGHEST)  53.6 us
    another operation x30, local copies, waits for them, and re-layouts, spread_face(): jnp.tile(rows, (1,) * len(lead) + (1, brick)).reshape(lead + (brick ** 3,))  45.6 us
    dot_general x10, matrix products, face_layer(): return jnp.dot(field, x_table(side, brick), precision=lax.Precision.HIGHEST)  26.2 us
    ppermute x5, starting transfers between devices, extended(): before = lax.ppermute(last, axis, up)  17.9 us
    gather x20, local copies, waits for them, and re-layouts, neighbour_faces(): jnp.take(face_layer(field, side ^ 1, BRICK_EDGE_VOXELS), plan['places'][s...  13.3 us
    select_n x25, other arithmetic, neighbour_faces(): faces.append(jnp.where(plan['valid'][side][:, None], picked, fill))  10.5 us
  transfers between devices with their start and end apart: 10, of which 0 were waited for; matrix products, arithmetic and copies ran while one was open for 20% of the time, Pallas kernels for 0%

commit v1 on v0

v1 whole, which is shorter than its diff:
```python
import functools

import jax
import jax.numpy as jnp
from jax import lax
from jax.experimental import pallas as pl
from jax.experimental.pallas import tpu as pltpu
from jax.sharding import PartitionSpec as P

EDGE = 16
ITERS = 4
LANES = 128
SLOTS = 8
TILES = EDGE**3 // LANES
HALF = EDGE // 2
MOMENTS = 2 * ITERS
MESH = pl.DeviceIdType.MESH


def pick(tile, index):
    return jnp.take_along_axis(tile, index, axis=0, mode="promise_in_bounds")


def total_of(terms):
    terms = list(terms)
    while len(terms) > 1:
        terms = [
            terms[i] + terms[i + 1] if i + 1 < len(terms) else terms[i]
            for i in range(0, len(terms), 2)
        ]
    return terms[0]


def cg_coefficients(nu):
    def gram(i, j):
        return 0.5 * (nu[i + j] + nu[abs(i - j)])

    def pair(a, b):
        return total_of(x * y * gram(i, j) for i, x in enumerate(a) for j, y in enumerate(b))

    def image_of(p):
        q = list(p) + [jnp.zeros_like(p[0])]
        for j, x in enumerate(p):
            if j == 0:
                q[1] = q[1] - x
            else:
                q[j + 1] = q[j + 1] - 0.5 * x
                q[j - 1] = q[j - 1] - 0.5 * x
        return q

    scaled = [jnp.ones_like(nu[0])]
    direction = list(scaled)
    iterate = []
    current = nu[0]
    for step in range(ITERS):
        image = image_of(direction)
        alpha = current / pair(direction, image)
        iterate = [
            (iterate[i] + alpha * x) if i < len(iterate) else alpha * x
            for i, x in enumerate(direction)
        ]
        scaled = [
            (scaled[i] - alpha * x) if i < len(scaled) else -alpha * x
            for i, x in enumerate(image)
        ]
        if step + 1 < ITERS:
            fresh = pair(scaled, scaled)
            beta = fresh / current
            direction = [
                x + beta * direction[i] if i < len(direction) else x
                for i, x in enumerate(scaled)
            ]
            current = fresh
    return iterate, scaled


def kernel(
    peers, subs, k_ref, nb_ref, live_ref, x_ref, r_ref,
    kp, field, weight, diag, link, faces, ghosts, fix, edge_w, moments, gathered,
    face_send, face_recv, sum_send, sum_recv,
):
    me = lax.axis_index("curve") * subs + lax.axis_index("sub")

    def device(index):
        return {"curve": index // subs, "sub": lax.rem(index, subs)}

    barrier = pltpu.get_barrier_semaphore()

    def greet(offset, carry):
        pl.semaphore_signal(
            barrier, inc=1, device_id=device(lax.rem(me + offset, peers)), device_id_type=MESH
        )
        return carry

    lax.fori_loop(1, peers, greet, 0)

    shape = (SLOTS, LANES)
    lane = lax.broadcasted_iota(jnp.int32, shape, 1)
    slot = lax.broadcasted_iota(jnp.int32, shape, 0)
    column = lane % EDGE
    first_x, last_x = column == 0, column == EDGE - 1
    first_y, last_y = lane < EDGE, lane >= LANES - EDGE
    live = slot < live_ref[0]
    index, valid, remote = [], [], []
    for side in range(6):
        entry = jnp.full(shape, nb_ref[side, 0], jnp.int32)
        for s in range(1, SLOTS):
            entry = jnp.where(slot == s, nb_ref[side, s], entry)
        valid.append(entry >= 0)
        index.append(jnp.where(valid[side], entry % SLOTS, 0))
        if side < 2:
            remote.append(
                valid[side] & ((entry < me * SLOTS) | (entry >= (me + 1) * SLOTS))
            )

    def copies(step, width):
        def make(side, peer):
            span = pl.ds(0, width)
            return pltpu.make_async_remote_copy(
                src_ref=faces.at[step, side, span],
                dst_ref=ghosts.at[step, 1 - side, span],
                send_sem=face_send.at[step, side],
                recv_sem=face_recv.at[step, 1 - side],
                device_id=device(peer),
                device_id_type=MESH,
            )

        return make(0, jnp.maximum(me - 1, 0)), make(1, jnp.minimum(me + 1, peers - 1))

    def send(step, width):
        down, up = copies(step, width)

        @pl.when(me > 0)
        def _():
            down.start()

        @pl.when(me < peers - 1)
        def _():
            up.start()

    def receive(step, width):
        down, up = copies(step, width)

        @pl.when(me < peers - 1)
        def _():
            down.wait_recv()
            up.wait_send()

        @pl.when(me > 0)
        def _():
            up.wait_recv()
            down.wait_send()

    def compact(tile, side, place, into):
        turn = place if side == 0 else place + LANES - (EDGE - 1)
        return jnp.where(column == place, pltpu.roll(tile, lax.rem(turn, LANES), 1), into)

    def spread(tile, side, place):
        turn = (LANES - place) if side == 0 else (EDGE - 1) - place
        return pltpu.roll(tile, lax.rem(turn + LANES, LANES), 1)

    def ghost(step, side, comp, half):
        near = pick(faces[step, 1 - side, comp, half], index[side])
        far = pick(ghosts[step, side, comp, half], index[side])
        return jnp.where(remote[side], far, near)

    def shifts_y(pair):
        low = [pltpu.roll(tile, EDGE, 1) for tile in pair]
        high = [pltpu.roll(tile, LANES - EDGE, 1) for tile in pair]
        before = [
            jnp.where(first_y, pick(low[1], index[2]), low[0]),
            jnp.where(first_y, low[0], low[1]),
        ]
        after = [
            jnp.where(last_y, high[1], high[0]),
            jnp.where(last_y, pick(high[0], index[3]), high[1]),
        ]
        return before, after

    zero = jnp.zeros(shape, jnp.float32)

    for half in range(2):
        low, high = zero, zero
        for p in range(EDGE):
            t = half * EDGE + p
            tile = k_ref[:, t * LANES : (t + 1) * LANES]
            kp[2 + t] = tile
            low = compact(tile, 0, p, low)
            high = compact(tile, 1, p, high)
        faces[0, 0, 0, half] = low
        faces[0, 1, 0, half] = high
    for h in range(2):
        kp[h] = jnp.where(valid[4], pick(kp[TILES + h], index[4]), kp[2 + h])
        kp[TILES + 2 + h] = jnp.where(valid[5], pick(kp[2 + h], index[5]), kp[TILES + h])

    pl.semaphore_wait(barrier, peers - 1)
    send(0, 1)

    def harmonic(a, b):
        return jnp.where(live, 2.0 * a * b / (a + b), 0.0)

    def links(z, carry):
        pair = [kp[2 + 2 * z + h] for h in range(2)]
        before, after = shifts_y(pair)
        before[0] = jnp.where(first_y & ~valid[2], pair[0], before[0])
        after[1] = jnp.where(last_y & ~valid[3], pair[1], after[1])
        for h in range(2):
            t = 2 * z + h
            k = pair[h]
            link[0, t] = jnp.where(first_x, 0.0, harmonic(k, pltpu.roll(k, 1, 1)))
            link[1, t] = jnp.where(last_x, 0.0, harmonic(k, pltpu.roll(k, LANES - 1, 1)))
            link[2, t] = harmonic(k, before[h])
            link[3, t] = harmonic(k, after[h])
            link[4, t] = harmonic(k, kp[t])
            link[5, t] = harmonic(k, kp[t + 4])
        return carry

    lax.fori_loop(0, EDGE, links, 0)
    receive(0, 1)

    for side in range(2):
        for half in range(2):
            own = faces[0, side, 0, half]
            other = jnp.where(valid[side], ghost(0, side, 0, half), own)
            fix[side, 0, half] = harmonic(own, other)

    def finish_faces(step, half, found):
        for side in range(2):
            for comp in range(3):
                faces[step, side, comp, half] = found[side * 3 + comp]

    for half in range(2):

        def start(row, carry, half=half):
            carry = list(carry)
            for h in range(2):
                p = 2 * row + h
                t = half * EDGE + p
                w = [link[side, t] for side in range(6)]
                w[0] = jnp.where(first_x, spread(fix[0, 0, half], 0, p), w[0])
                w[1] = jnp.where(last_x, spread(fix[1, 0, half], 1, p), w[1])
                total = ((((w[0] + w[1]) + w[2]) + w[3]) + w[4]) + w[5]
                d = jnp.where(live, total, 1.0)
                inverse = 1.0 / d
                diag[t] = d
                n = [x * inverse for x in w]
                if h == 0:
                    n[2] = jnp.where(first_y & ~valid[2], 0.0, n[2])
                if h == 1:
                    n[3] = jnp.where(last_y & ~valid[3], 0.0, n[3])
                weight[0, t] = jnp.where(first_x, 0.0, n[0])
                weight[1, t] = jnp.where(last_x, 0.0, n[1])
                for side in range(2, 6):
                    weight[side, t] = n[side]
                for comp in range(3):
                    v = (w[2 * comp + 1] - w[2 * comp]) * inverse
                    field[0, comp, 2 + t] = v
                    carry[comp] = compact(v, 0, p, carry[comp])
                    carry[3 + comp] = compact(v, 1, p, carry[3 + comp])
                carry[6] = compact(n[0], 0, p, carry[6])
                carry[7] = compact(n[1], 1, p, carry[7])
            return tuple(carry)

        found = lax.fori_loop(0, HALF, start, (zero,) * 8)
        finish_faces(1, half, found)
        edge_w[0, half] = jnp.where(valid[0], found[6], 0.0)
        edge_w[1, half] = jnp.where(valid[1], found[7], 0.0)

    sums = []
    for j in range(ITERS):
        if j == 0:
            send(1, 3)
        for comp in range(3):
            for h in range(2):
                field[j, comp, h] = jnp.where(
                    valid[4], pick(field[j, comp, TILES + h], index[4]), 0.0
                )
                field[j, comp, TILES + 2 + h] = jnp.where(
                    valid[5], pick(field[j, comp, 2 + h], index[5]), 0.0
                )
        for half in range(2):

            def inner(row, carry, half=half, j=j):
                carry = list(carry)
                base = half * EDGE + 2 * row
                w = [[weight[side, base + h] for side in range(6)] for h in range(2)]
                for comp in range(3):
                    pair = [field[j, comp, 2 + base + h] for h in range(2)]
                    before, after = shifts_y(pair)
                    for h in range(2):
                        t = base + h
                        p = 2 * row + h
                        u = pair[h]
                        value = (
                            (w[h][0] * pltpu.roll(u, 1, 1) + w[h][1] * pltpu.roll(u, LANES - 1, 1))
                            + (w[h][2] * before[h] + w[h][3] * after[h])
                            + (w[h][4] * field[j, comp, t] + w[h][5] * field[j, comp, t + 4])
                        )
                        if j > 0:
                            value = 2.0 * value - field[j - 1, comp, 2 + t]
                        field[j + 1, comp, 2 + t] = value
                        if j + 1 < ITERS:
                            carry[comp] = compact(value, 0, p, carry[comp])
                            carry[3 + comp] = compact(value, 1, p, carry[3 + comp])
                return tuple(carry)

            found = lax.fori_loop(0, HALF, inner, (zero,) * 6)
            if j + 1 < ITERS:
                finish_faces(j + 2, half, found)
        receive(j + 1, 3)
        for half in range(2):
            for side in range(2):
                w = edge_w[side, half]
                if j > 0:
                    w = 2.0 * w
                for comp in range(3):
                    extra = jnp.where(valid[side], w * ghost(j + 1, side, comp, half), 0.0)
                    fix[side, comp, half] = extra
                    if j + 1 < ITERS:
                        faces[j + 2, side, comp, half] = faces[j + 2, side, comp, half] + extra
        if j + 1 < ITERS:
            send(j + 2, 3)

        accumulated = (zero,) * 6
        for half in range(2):

            def outer(row, carry, half=half, j=j):
                carry = list(carry)
                for h in range(2):
                    p = 2 * row + h
                    t = half * EDGE + p
                    d = diag[t]
                    for comp in range(3):
                        value = field[j + 1, comp, 2 + t]
                        value = value + jnp.where(
                            first_x,
                            spread(fix[0, comp, half], 0, p),
                            jnp.where(last_x, spread(fix[1, comp, half], 1, p), 0.0),
                        )
                        field[j + 1, comp, 2 + t] = value
                        old = field[j, comp, 2 + t]
                        scaled = d * old
                        carry[comp] = carry[comp] + scaled * old
                        carry[3 + comp] = carry[3 + comp] + scaled * value
                return tuple(carry)

            accumulated = lax.fori_loop(0, HALF, outer, accumulated)
        sums.append(accumulated)

    mine = zero
    for comp in range(3):
        rows = zero
        for j in range(ITERS):
            for odd in range(2):
                row = jnp.sum(sums[j][3 * odd + comp], axis=0, keepdims=True)
                rows = jnp.where(slot == 2 * j + odd, row, rows)
        mine = jnp.where(lane == comp, jnp.sum(rows, axis=1, keepdims=True), mine)
    moments[...] = mine
    gathered[me] = mine

    def share(offset):
        peer = lax.rem(me + offset, peers)
        return pltpu.make_async_remote_copy(
            src_ref=moments,
            dst_ref=gathered.at[me],
            send_sem=sum_send.at[offset],
            recv_sem=sum_recv.at[me],
            device_id=device(peer),
            device_id_type=MESH,
        )

    def launch(offset, carry):
        share(offset).start()
        return carry

    lax.fori_loop(1, peers, launch, 0)

    def collect(offset, carry):
        source = lax.rem(me + offset, peers)
        share(offset).wait_send()
        pltpu.make_async_remote_copy(
            src_ref=moments,
            dst_ref=gathered.at[source],
            send_sem=sum_send.at[offset],
            recv_sem=sum_recv.at[source],
            device_id=device(source),
            device_id_type=MESH,
        ).wait_recv()
        return carry

    lax.fori_loop(1, peers, collect, 0)
    whole = jnp.sum(gathered[...], axis=0)

    rows = [whole[m : m + 1, :] for m in range(MOMENTS)]
    nu = rows[:2]
    for m in range(2, MOMENTS):
        nu.append(2.0 * rows[m] - rows[m % 2])
    iterate, scaled = cg_coefficients(nu)

    def over(row, comp):
        return jnp.broadcast_to(row[:, comp : comp + 1], shape)

    for comp in range(3):
        a = [over(row, comp) for row in iterate]
        b = [over(row, comp) for row in scaled]
        for t in range(TILES):
            v = [field[j, comp, 2 + t] for j in range(ITERS + 1)]
            span = slice(t * LANES, (t + 1) * LANES)
            x_ref[comp, :, span] = total_of(a[j] * v[j] for j in range(ITERS))
            r_ref[comp, :, span] = diag[t] * total_of(b[j] * v[j] for j in range(ITERS + 1))


def local(peers, subs, conductivity, neighbours, live_count):
    slots, voxels = conductivity.shape
    out = jax.ShapeDtypeStruct((3, slots, voxels), jnp.float32)
    vmem = pl.BlockSpec(memory_space=pltpu.VMEM)
    smem = pl.BlockSpec(memory_space=pltpu.SMEM)
    tile = (SLOTS, LANES)
    return pl.pallas_call(
        functools.partial(kernel, peers, subs),
        out_shape=(out, out),
        in_specs=[vmem, smem, smem],
        out_specs=(vmem, vmem),
        scratch_shapes=[
            pltpu.VMEM((TILES + 4, *tile), jnp.float32),
            pltpu.VMEM((ITERS + 1, 3, TILES + 4, *tile), jnp.float32),
            pltpu.VMEM((6, TILES, *tile), jnp.float32),
            pltpu.VMEM((TILES, *tile), jnp.float32),
            pltpu.VMEM((6, TILES, *tile), jnp.float32),
            pltpu.VMEM((ITERS + 1, 2, 3, 2, *tile), jnp.float32),
            pltpu.VMEM((ITERS + 1, 2, 3, 2, *tile), jnp.float32),
            pltpu.VMEM((2, 3, 2, *tile), jnp.float32),
            pltpu.VMEM((2, 2, *tile), jnp.float32),
            pltpu.VMEM(tile, jnp.float32),
            pltpu.VMEM((peers, *tile), jnp.float32),
            pltpu.SemaphoreType.DMA((ITERS + 1, 2)),
            pltpu.SemaphoreType.DMA((ITERS + 1, 2)),
            pltpu.SemaphoreType.DMA((peers,)),
            pltpu.SemaphoreType.DMA((peers,)),
        ],
        compiler_params=pltpu.CompilerParams(
            collective_id=0, has_side_effects=True, vmem_limit_bytes=24 * 1024 * 1024
        ),
    )(conductivity, neighbours, live_count)


def solution(mesh):
    names = ("ens", "curve", "sub")
    peers = mesh.shape["curve"] * mesh.shape["sub"]
    in_specs = (P(names, None), P(None, names), P(names))
    out_specs = (P(None, names, None), P(None, names, None))
    return jax.shard_map(
        functools.partial(local, peers, mesh.shape["sub"]),
        mesh=mesh, in_specs=in_specs, out_specs=out_specs, check_vma=False,
    )
```

time: 440 us -> 35.5 us (0.08); the launches traced: 435 us -> 35.3 us
  blocking collectives: 214 us -> 0 us
  local copies, waits for them, and re-layouts: 88.5 us -> 3.08 us
  matrix products: 79.8 us -> 0 us
  Pallas kernels: 0 us -> 31 us
  starting transfers between devices: 24.8 us -> 0 us
  other arithmetic: 23 us -> 0 us
    psum x7 -> x0, blocking collectives: 214 us -> none  [the longest x4 123 us: residual_product(): return lax.psum(jnp.sum(residual * scaled, axis=(1, 2)), ('curve', 'sub'))]
    dot_general x20 -> x0, matrix products: 79.8 us -> none  [the longest x10 53.6 us: spread_face(): jnp.dot(face, x_table(side, brick).T, precision=lax.Precision.HIGHEST)]
    another operation x43 -> x0, local copies, waits for them, and re-layouts: 46.7 us -> none  [the longest x30 45.6 us: spread_face(): jnp.tile(rows, (1,) * len(lead) + (1, brick)).reshape(lead + (brick ** 3,))]
    pallas_call x0 -> x1, Pallas kernels: none -> 31 us  [local(): pl.pallas_call(functools.partial(kernel, peers, subs), out_shape=(out, ou...]
    ppermute x10 -> x0, starting transfers between devices: 24.8 us -> none  [the longest x5 17.9 us: extended(): before = lax.ppermute(last, axis, up)]
    gather x30 -> x0, local copies, waits for them, and re-layouts: 20 us -> none  [the longest x20 13.3 us: neighbour_faces(): jnp.take(face_layer(field, side ^ 1, BRICK_EDGE_VOXELS), plan['places'][s...]
    slice x33 -> x0, local copies, waits for them, and re-layouts: 14.1 us -> none  [the longest x8 6.83 us: inner_shift(): lax.slice_in_dim(field, 0, total - stride, axis=last)]
    select_n x25 -> x0, other arithmetic: 10.5 us -> none  [neighbour_faces(): faces.append(jnp.where(plan['valid'][side][:, None], picked, fill))]
  transfers between devices with their start and end apart: 10 -> 0, of which waited for: 0 -> 0; matrix products, arithmetic and copies ran while one was open for 20% -> 0% of each run, Pallas kernels for 0% -> 0%
where the time goes in v1:
time: 35.5 us; the launch traced here: 35.3 us
  Pallas kernels  31 us (87%)
  local copies, waits for them, and re-layouts  3.08 us (9%)
  between operations  1.29 us (4%)
    pallas_call x1, Pallas kernels, local(): pl.pallas_call(functools.partial(kernel, peers, subs), out_shape=(out, ou...  31 us
    unnamed x6, local copies, waits for them, and re-layouts  3.08 us

profile of v1, /device:TPU:0, one launch (start us, length us, event | category | flops | bytes accessed | tf_op | source)
XLA Modules:
  0.0 35.3 jit_solution(6533529371486538652)
XLA Ops:
  1.3 0.0 copy-start
  1.3 0.9 %copy-done = f32[8,4096]{1,0:T(8,128)S(1)} copy-done((f32[8,4096]{1,0:T(8,128)S(1)}, f32[8,4096]{1,0:T(8,128)}, u32[]{:S(2)}) %copy-start) | copy-done | bytes 131096
  2.2 0.0 copy-start.1
  2.2 0.7 %copy-done.1 = s32[6,8]{1,0:T(8,128)S(1)} copy-done((s32[6,8]{1,0:T(8,128)S(1)}, s32[6,8]{1,0:T(8,128)}, u32[]{:S(2)}) %copy-start.1) | copy-done | bytes 216
  2.9 31.0 %shard_map.50 = (f32[3,8,4096]{2,1,0:T(8,128)S(1)}, f32[3,8,4096]{2,1,0:T(8,128)S(1)}) custom-call(f32[8,4096]{1,0:T(8,128)S(1)} %copy-done, s32[6,8]{1,0:T(8,128)S(1)} %copy-done.1, s32[1]{0:T(128)S(6)} %copy.7.live_ref), custom_call_target="tpu_custom_call" | custom-call | tf_op jit(solution)/shard_map/pallas_call | solution.py:419
  33.8 0.7 %copy.8 = f32[3,8,4096]{2,1,0:T(8,128)} copy(f32[3,8,4096]{2,1,0:T(8,128)S(1)} %get-tuple-element.4) | data formatting | bytes 786432
  34.6 0.7 %copy.9 = f32[3,8,4096]{2,1,0:T(8,128)} copy(f32[3,8,4096]{2,1,0:T(8,128)S(1)} %get-tuple-element.5) | data formatting | bytes 786432
Async XLA Ops:
  1.3 0.9 %copy-start = (f32[8,4096]{1,0:T(8,128)S(1)}, f32[8,4096]{1,0:T(8,128)}, u32[]{:S(2)}) copy-start(f32[8,4096]{1,0:T(8,128)} %k_ref.1) | copy-start | bytes 393220
  2.2 0.7 %copy-start.1 = (s32[6,8]{1,0:T(8,128)S(1)}, s32[6,8]{1,0:T(8,128)}, u32[]{:S(2)}) copy-start(s32[6,8]{1,0:T(8,128)} %nb_ref.1) | copy-start | bytes 580

commit v2 on v1

v2 whole, which is shorter than its diff:
```python
import functools

import jax
import jax.numpy as jnp
from jax import lax
from jax.experimental import pallas as pl
from jax.experimental.pallas import tpu as pltpu
from jax.sharding import PartitionSpec as P

EDGE = 16
ITERS = 4
LANES = 128
SLOTS = 8
MOMENTS = 2 * ITERS
MESH = pl.DeviceIdType.MESH


def total_of(terms):
    terms = list(terms)
    while len(terms) > 1:
        terms = [
            terms[i] + terms[i + 1] if i + 1 < len(terms) else terms[i]
            for i in range(0, len(terms), 2)
        ]
    return terms[0]


def cg_coefficients(nu):
    def gram(i, j):
        return 0.5 * (nu[i + j] + nu[abs(i - j)])

    def pair(a, b):
        return total_of(x * y * gram(i, j) for i, x in enumerate(a) for j, y in enumerate(b))

    def image_of(p):
        q = list(p) + [jnp.zeros_like(p[0])]
        for j, x in enumerate(p):
            if j == 0:
                q[1] = q[1] - x
            else:
                q[j + 1] = q[j + 1] - 0.5 * x
                q[j - 1] = q[j - 1] - 0.5 * x
        return q

    scaled = [jnp.ones_like(nu[0])]
    direction = list(scaled)
    iterate = []
    current = nu[0]
    for step in range(ITERS):
        image = image_of(direction)
        alpha = current / pair(direction, image)
        iterate = [
            (iterate[i] + alpha * x) if i < len(iterate) else alpha * x
            for i, x in enumerate(direction)
        ]
        scaled = [
            (scaled[i] - alpha * x) if i < len(scaled) else -alpha * x
            for i, x in enumerate(image)
        ]
        if step + 1 < ITERS:
            fresh = pair(scaled, scaled)
            beta = fresh / current
            direction = [
                x + beta * direction[i] if i < len(direction) else x
                for i, x in enumerate(scaled)
            ]
            current = fresh
    return iterate, scaled


def kernel(
    peers, subs, k_ref, nb_ref, live_ref, x_ref, r_ref,
    kp, field, weight, diag, link, faces, ghosts, edge_w, turned, moments, gathered,
    face_send, face_recv, sum_send, sum_recv,
):
    me = lax.axis_index("curve") * subs + lax.axis_index("sub")

    def device(index):
        return {"curve": index // subs, "sub": lax.rem(index, subs)}

    barrier = pltpu.get_barrier_semaphore()

    def greet(offset, carry):
        pl.semaphore_signal(
            barrier, inc=1, device_id=device(lax.rem(me + offset, peers)), device_id_type=MESH
        )
        return carry

    lax.fori_loop(1, peers, greet, 0)

    shape = (EDGE, LANES)
    lane = lax.broadcasted_iota(jnp.int32, shape, 1)
    row = lax.broadcasted_iota(jnp.int32, shape, 0)
    depth = lane % EDGE
    owner = lane // EDGE
    first_x, last_x = row == 0, row == EDGE - 1
    first_z, last_z = depth == 0, depth == EDGE - 1
    live = owner < live_ref[0]
    index, valid, remote = [], [], []
    for side in range(6):
        entry = jnp.full(shape, nb_ref[side, 0], jnp.int32)
        for s in range(1, SLOTS):
            entry = jnp.where(owner == s, nb_ref[side, s], entry)
        valid.append(entry >= 0)
        index.append(jnp.where(valid[side], entry % SLOTS, 0) * EDGE)
        if side < 2:
            remote.append(
                valid[side] & ((entry < me * SLOTS) | (entry >= (me + 1) * SLOTS))
            )
    for side in range(4):
        index[side] = index[side] + depth
    index[4] = jnp.where(first_z, index[4] + (EDGE - 1), lane - 1)
    index[5] = jnp.where(last_z, index[5], lane + 1)

    def pick(block, side):
        where = index[side]
        return jnp.concatenate(
            [
                jnp.take_along_axis(
                    block[h : h + 8], where[h : h + 8], axis=1, mode="promise_in_bounds"
                )
                for h in range(0, EDGE, 8)
            ],
            axis=0,
        )

    def copies(step, width):
        def make(side, peer):
            span = pl.ds(0, width)
            return pltpu.make_async_remote_copy(
                src_ref=faces.at[step, side, span],
                dst_ref=ghosts.at[step, 1 - side, span],
                send_sem=face_send.at[step, side],
                recv_sem=face_recv.at[step, 1 - side],
                device_id=device(peer),
                device_id_type=MESH,
            )

        return make(0, jnp.maximum(me - 1, 0)), make(1, jnp.minimum(me + 1, peers - 1))

    def send(step, width):
        down, up = copies(step, width)

        @pl.when(me > 0)
        def _():
            down.start()

        @pl.when(me < peers - 1)
        def _():
            up.start()

    def receive(step, width):
        down, up = copies(step, width)

        @pl.when(me < peers - 1)
        def _():
            down.wait_recv()
            up.wait_send()

        @pl.when(me > 0)
        def _():
            up.wait_recv()
            down.wait_send()

    def layer(side, pad):
        return pl.ds(pad + (EDGE - 1) * side, EDGE, stride=EDGE)

    def ghost(step, side, comp):
        near = pick(faces[step, 1 - side, comp], side)
        far = pick(ghosts[step, side, comp], side)
        return jnp.where(remote[side], far, near)

    def block_of(y, ahead=0):
        start = (y + 1) * EDGE + ahead
        return pl.ds(start, EDGE)

    zero = jnp.zeros(shape, jnp.float32)
    end = EDGE * EDGE

    for h in range(2):
        for z in range(EDGE):
            at = z * EDGE * EDGE + h * LANES
            turned[0, h, pl.ds(z, SLOTS, stride=EDGE), :] = k_ref[:, at : at + LANES]
        kp[EDGE + h * LANES : EDGE + (h + 1) * LANES] = turned[0, h].T
    for side in range(2):
        faces[0, side, 0] = kp[layer(side, EDGE), :]
    lower, upper = kp[EDGE : 2 * EDGE], kp[end : end + EDGE]
    kp[0:EDGE] = jnp.where(valid[2], pick(upper, 2), lower)
    kp[end + EDGE : end + 2 * EDGE] = jnp.where(valid[3], pick(lower, 3), upper)

    pl.semaphore_wait(barrier, peers - 1)
    send(0, 1)

    def harmonic(a, b):
        return jnp.where(live, 2.0 * a * b / (a + b), 0.0)

    def links(y, carry):
        k = kp[block_of(y), :]
        here = pl.ds(y * EDGE, EDGE)
        link[0, here, :] = harmonic(k, kp[block_of(y, -1), :])
        link[1, here, :] = harmonic(k, kp[block_of(y, 1), :])
        link[2, here, :] = harmonic(k, kp[pl.ds(y * EDGE, EDGE), :])
        link[3, here, :] = harmonic(k, kp[block_of(y + 1), :])
        link[4, here, :] = harmonic(k, jnp.where(first_z & ~valid[4], k, pick(k, 4)))
        link[5, here, :] = harmonic(k, jnp.where(last_z & ~valid[5], k, pick(k, 5)))
        return carry

    lax.fori_loop(0, EDGE, links, 0)
    receive(0, 1)

    for side in range(2):
        own = faces[0, side, 0]
        other = jnp.where(valid[side], ghost(0, side, 0), own)
        link[side, layer(side, 0), :] = harmonic(own, other)

    def begin(y, carry):
        here = pl.ds(y * EDGE, EDGE)
        w = [link[side, here, :] for side in range(6)]
        total = ((((w[0] + w[1]) + w[2]) + w[3]) + w[4]) + w[5]
        d = jnp.where(live, total, 1.0)
        inverse = 1.0 / d
        diag[here, :] = d
        n = [x * inverse for x in w]
        n[4] = jnp.where(first_z & ~valid[4], 0.0, n[4])
        n[5] = jnp.where(last_z & ~valid[5], 0.0, n[5])
        for side in range(6):
            weight[side, here, :] = n[side]
        for comp in range(3):
            field[0, comp, block_of(y), :] = (w[2 * comp + 1] - w[2 * comp]) * inverse
        return carry

    lax.fori_loop(0, EDGE, begin, 0)
    for side in range(2):
        edge_w[side] = jnp.where(valid[side], weight[side, layer(side, 0), :], 0.0)
        weight[side, layer(side, 0), :] = zero
        for comp in range(3):
            faces[1, side, comp] = field[0, comp, layer(side, EDGE), :]
    send(1, 3)

    sums = []
    for j in range(ITERS):
        for comp in range(3):
            field[j, comp, 0:EDGE] = jnp.where(
                valid[2], pick(field[j, comp, end : end + EDGE], 2), 0.0
            )
            field[j, comp, end + EDGE : end + 2 * EDGE] = jnp.where(
                valid[3], pick(field[j, comp, EDGE : 2 * EDGE], 3), 0.0
            )

        def inner(y, carry, j=j):
            carry = list(carry)
            here = pl.ds(y * EDGE, EDGE)
            w = [weight[side, here, :] for side in range(6)]
            d = diag[here, :]
            for comp in range(3):
                u = field[j, comp, block_of(y), :]
                value = (
                    (w[0] * field[j, comp, block_of(y, -1), :]
                     + w[1] * field[j, comp, block_of(y, 1), :])
                    + (w[2] * field[j, comp, pl.ds(y * EDGE, EDGE), :]
                       + w[3] * field[j, comp, block_of(y + 1), :])
                    + (w[4] * pick(u, 4) + w[5] * pick(u, 5))
                )
                scaled = d * u
                carry[comp] = carry[comp] + scaled * u
                if j > 0:
                    old = field[j - 1, comp, block_of(y), :]
                    value = 2.0 * value - old
                    carry[3 + comp] = carry[3 + comp] + scaled * old
                field[j + 1, comp, block_of(y), :] = value
            return tuple(carry)

        sums.append(lax.fori_loop(0, EDGE, inner, (zero,) * 6))
        receive(j + 1, 3)
        for side in range(2):
            w = edge_w[side]
            if j > 0:
                w = 2.0 * w
            for comp in range(3):
                extra = jnp.where(valid[side], w * ghost(j + 1, side, comp), 0.0)
                found = field[j + 1, comp, layer(side, EDGE), :] + extra
                field[j + 1, comp, layer(side, EDGE), :] = found
                if j + 1 < ITERS:
                    faces[j + 2, side, comp] = found
        if j + 1 < ITERS:
            send(j + 2, 3)

    def last(y, carry):
        d = diag[pl.ds(y * EDGE, EDGE), :]
        return tuple(
            carry[comp]
            + d * field[ITERS - 1, comp, block_of(y), :] * field[ITERS, comp, block_of(y), :]
            for comp in range(3)
        )

    final = lax.fori_loop(0, EDGE, last, (zero,) * 3)

    def summed(j, odd, comp):
        if not odd:
            return sums[j][comp]
        return sums[j + 1][3 + comp] if j + 1 < ITERS else final[comp]

    shape = (SLOTS, LANES)
    lane = lax.broadcasted_iota(jnp.int32, shape, 1)
    slot = lax.broadcasted_iota(jnp.int32, shape, 0)
    zero = jnp.zeros(shape, jnp.float32)
    mine = zero
    for comp in range(3):
        rows = zero
        for j in range(ITERS):
            for odd in range(2):
                row = jnp.sum(summed(j, odd, comp), axis=0, keepdims=True)
                rows = jnp.where(slot == 2 * j + odd, row, rows)
        mine = jnp.where(lane == comp, jnp.sum(rows, axis=1, keepdims=True), mine)
    moments[...] = mine
    gathered[me] = mine

    def share(offset):
        peer = lax.rem(me + offset, peers)
        return pltpu.make_async_remote_copy(
            src_ref=moments,
            dst_ref=gathered.at[me],
            send_sem=sum_send.at[offset],
            recv_sem=sum_recv.at[me],
            device_id=device(peer),
            device_id_type=MESH,
        )

    def launch(offset, carry):
        share(offset).start()
        return carry

    lax.fori_loop(1, peers, launch, 0)

    def collect(offset, carry):
        source = lax.rem(me + offset, peers)
        share(offset).wait_send()
        pltpu.make_async_remote_copy(
            src_ref=moments,
            dst_ref=gathered.at[source],
            send_sem=sum_send.at[offset],
            recv_sem=sum_recv.at[source],
            device_id=device(source),
            device_id_type=MESH,
        ).wait_recv()
        return carry

    lax.fori_loop(1, peers, collect, 0)
    whole = jnp.sum(gathered[...], axis=0)

    rows = [whole[m : m + 1, :] for m in range(MOMENTS)]
    nu = rows[:2]
    for m in range(2, MOMENTS):
        nu.append(2.0 * rows[m] - rows[m % 2])
    iterate, scaled = cg_coefficients(nu)

    def over(row, comp):
        return jnp.broadcast_to(row[:, comp : comp + 1], (1, LANES))

    for comp in range(3):
        a = [over(row, comp) for row in iterate]
        b = [over(row, comp) for row in scaled]
        for h in range(2):
            inside = pl.ds(EDGE + h * LANES, LANES)
            v = [field[j, comp, inside, :] for j in range(ITERS + 1)]
            d = diag[pl.ds(h * LANES, LANES), :]
            turned[comp, h] = total_of(a[j] * v[j] for j in range(ITERS)).T
            turned[3 + comp, h] = (d * total_of(b[j] * v[j] for j in range(ITERS + 1))).T
            for z in range(EDGE):
                at = z * EDGE * EDGE + h * LANES
                strip = pl.ds(z, SLOTS, stride=EDGE)
                x_ref[comp, :, at : at + LANES] = turned[comp, h, strip, :]
                r_ref[comp, :, at : at + LANES] = turned[3 + comp, h, strip, :]


def local(peers, subs, conductivity, neighbours, live_count):
    slots, voxels = conductivity.shape
    out = jax.ShapeDtypeStruct((3, slots, voxels), jnp.float32)
    vmem = pl.BlockSpec(memory_space=pltpu.VMEM)
    smem = pl.BlockSpec(memory_space=pltpu.SMEM)
    tile = (SLOTS, LANES)
    rows = EDGE * EDGE
    return pl.pallas_call(
        functools.partial(kernel, peers, subs),
        out_shape=(out, out),
        in_specs=[vmem, smem, smem],
        out_specs=(vmem, vmem),
        scratch_shapes=[
            pltpu.VMEM((rows + 2 * EDGE, LANES), jnp.float32),
            pltpu.VMEM((ITERS + 1, 3, rows + 2 * EDGE, LANES), jnp.float32),
            pltpu.VMEM((6, rows, LANES), jnp.float32),
            pltpu.VMEM((rows, LANES), jnp.float32),
            pltpu.VMEM((6, rows, LANES), jnp.float32),
            pltpu.VMEM((ITERS + 1, 2, 3, EDGE, LANES), jnp.float32),
            pltpu.VMEM((ITERS + 1, 2, 3, EDGE, LANES), jnp.float32),
            pltpu.VMEM((2, EDGE, LANES), jnp.float32),
            pltpu.VMEM((6, 2, LANES, LANES), jnp.float32),
            pltpu.VMEM(tile, jnp.float32),
            pltpu.VMEM((peers, *tile), jnp.float32),
            pltpu.SemaphoreType.DMA((ITERS + 1, 2)),
            pltpu.SemaphoreType.DMA((ITERS + 1, 2)),
            pltpu.SemaphoreType.DMA((peers,)),
            pltpu.SemaphoreType.DMA((peers,)),
        ],
        compiler_params=pltpu.CompilerParams(
            collective_id=0, has_side_effects=True, vmem_limit_bytes=24 * 1024 * 1024
        ),
    )(conductivity, neighbours, live_count)


def solution(mesh):
    names = ("ens", "curve", "sub")
    peers = mesh.shape["curve"] * mesh.shape["sub"]
    in_specs = (P(names, None), P(None, names), P(names))
    out_specs = (P(None, names, None), P(None, names, None))
    return jax.shard_map(
        functools.partial(local, peers, mesh.shape["sub"]),
        mesh=mesh, in_specs=in_specs, out_specs=out_specs, check_vma=False,
    )
```

time: 35.5 us -> 29.9 us (0.84)
  Pallas kernels: 31 us -> 25.3 us
    pallas_call x1, Pallas kernels: 31 us -> 25.3 us  [local(): pl.pallas_call(functools.partial(kernel, peers, subs), out_shape=(out, ou...]
where the time goes in v2:
time: 29.9 us; the launch traced here: 29.7 us
  Pallas kernels  25.3 us (85%)
  local copies, waits for them, and re-layouts  3.08 us (10%)
  between operations  1.29 us (4%)
    pallas_call x1, Pallas kernels, local(): pl.pallas_call(functools.partial(kernel, peers, subs), out_shape=(out, ou...  25.3 us
    unnamed x6, local copies, waits for them, and re-layouts  3.08 us

profile of v2, /device:TPU:0, one launch (start us, length us, event | category | flops | bytes accessed | tf_op | source)
XLA Modules:
  0.0 29.7 jit_solution(13739280072662527195)
XLA Ops:
  1.3 0.0 copy-start
  1.3 0.9 %copy-done = f32[8,4096]{1,0:T(8,128)S(1)} copy-done((f32[8,4096]{1,0:T(8,128)S(1)}, f32[8,4096]{1,0:T(8,128)}, u32[]{:S(2)}) %copy-start) | copy-done | bytes 131096
  2.2 0.0 copy-start.1
  2.2 0.7 %copy-done.1 = s32[6,8]{1,0:T(8,128)S(1)} copy-done((s32[6,8]{1,0:T(8,128)S(1)}, s32[6,8]{1,0:T(8,128)}, u32[]{:S(2)}) %copy-start.1) | copy-done | bytes 216
  2.9 25.3 %shard_map.50 = (f32[3,8,4096]{2,1,0:T(8,128)S(1)}, f32[3,8,4096]{2,1,0:T(8,128)S(1)}) custom-call(f32[8,4096]{1,0:T(8,128)S(1)} %copy-done, s32[6,8]{1,0:T(8,128)S(1)} %copy-done.1, s32[1]{0:T(128)S(6)} %copy.7.live_ref), custom_call_target="tpu_custom_call" | custom-call | tf_op jit(solution)/shard_map/pallas_call | solution.py:383
  28.2 0.7 %copy.8 = f32[3,8,4096]{2,1,0:T(8,128)} copy(f32[3,8,4096]{2,1,0:T(8,128)S(1)} %get-tuple-element.4) | data formatting | bytes 786432
  28.9 0.7 %copy.9 = f32[3,8,4096]{2,1,0:T(8,128)} copy(f32[3,8,4096]{2,1,0:T(8,128)S(1)} %get-tuple-element.5) | data formatting | bytes 786432
Async XLA Ops:
  1.3 0.9 %copy-start = (f32[8,4096]{1,0:T(8,128)S(1)}, f32[8,4096]{1,0:T(8,128)}, u32[]{:S(2)}) copy-start(f32[8,4096]{1,0:T(8,128)} %k_ref.1) | copy-start | bytes 393220
  2.2 0.7 %copy-start.1 = (s32[6,8]{1,0:T(8,128)S(1)}, s32[6,8]{1,0:T(8,128)}, u32[]{:S(2)}) copy-start(s32[6,8]{1,0:T(8,128)} %nb_ref.1) | copy-start | bytes 580

commit v3 on v2

--- a/solution.py
+++ b/solution.py
@@ -205,7 +205,7 @@
         link[5, here, :] = harmonic(k, jnp.where(last_z & ~valid[5], k, pick(k, 5)))
         return carry
 
-    lax.fori_loop(0, EDGE, links, 0)
+    lax.fori_loop(0, EDGE, links, 0, unroll=True)
     receive(0, 1)
 
     for side in range(2):
@@ -229,7 +229,7 @@
             field[0, comp, block_of(y), :] = (w[2 * comp + 1] - w[2 * comp]) * inverse
         return carry
 
-    lax.fori_loop(0, EDGE, begin, 0)
+    lax.fori_loop(0, EDGE, begin, 0, unroll=True)
     for side in range(2):
         edge_w[side] = jnp.where(valid[side], weight[side, layer(side, 0), :], 0.0)
         weight[side, layer(side, 0), :] = zero
@@ -270,7 +270,7 @@
                 field[j + 1, comp, block_of(y), :] = value
             return tuple(carry)
 
-        sums.append(lax.fori_loop(0, EDGE, inner, (zero,) * 6))
+        sums.append(lax.fori_loop(0, EDGE, inner, (zero,) * 6, unroll=True))
         receive(j + 1, 3)
         for side in range(2):
             w = edge_w[side]
@@ -293,7 +293,7 @@
             for comp in range(3)
         )
 
-    final = lax.fori_loop(0, EDGE, last, (zero,) * 3)
+    final = lax.fori_loop(0, EDGE, last, (zero,) * 3, unroll=True)
 
     def summed(j, odd, comp):
         if not odd:

time: 29.9 us -> 29.6 us (0.990)
  Pallas kernels: 25.3 us -> 25 us
where the time goes in v3:
time: 29.6 us; the launch traced here: 29.4 us
  Pallas kernels  25 us (84%)
  local copies, waits for them, and re-layouts  3.08 us (10%)
  between operations  1.29 us (4%)
    pallas_call x1, Pallas kernels, local(): pl.pallas_call(functools.partial(kernel, peers, subs), out_shape=(out, ou...  25 us
    unnamed x6, local copies, waits for them, and re-layouts  3.08 us

profile of v3, /device:TPU:0, one launch (start us, length us, event | category | flops | bytes accessed | tf_op | source)
XLA Modules:
  0.0 29.4 jit_solution(4357676713121324703)
XLA Ops:
  1.3 0.0 copy-start
  1.3 0.9 %copy-done = f32[8,4096]{1,0:T(8,128)S(1)} copy-done((f32[8,4096]{1,0:T(8,128)S(1)}, f32[8,4096]{1,0:T(8,128)}, u32[]{:S(2)}) %copy-start) | copy-done | bytes 131096
  2.2 0.0 copy-start.1
  2.2 0.7 %copy-done.1 = s32[6,8]{1,0:T(8,128)S(1)} copy-done((s32[6,8]{1,0:T(8,128)S(1)}, s32[6,8]{1,0:T(8,128)}, u32[]{:S(2)}) %copy-start.1) | copy-done | bytes 216
  2.9 25.0 %shard_map.50 = (f32[3,8,4096]{2,1,0:T(8,128)S(1)}, f32[3,8,4096]{2,1,0:T(8,128)S(1)}) custom-call(f32[8,4096]{1,0:T(8,128)S(1)} %copy-done, s32[6,8]{1,0:T(8,128)S(1)} %copy-done.1, s32[1]{0:T(128)S(6)} %copy.7.live_ref), custom_call_target="tpu_custom_call" | custom-call | tf_op jit(solution)/shard_map/pallas_call | solution.py:383
  27.9 0.7 %copy.8 = f32[3,8,4096]{2,1,0:T(8,128)} copy(f32[3,8,4096]{2,1,0:T(8,128)S(1)} %get-tuple-element.4) | data formatting | bytes 786432
  28.6 0.7 %copy.9 = f32[3,8,4096]{2,1,0:T(8,128)} copy(f32[3,8,4096]{2,1,0:T(8,128)S(1)} %get-tuple-element.5) | data formatting | bytes 786432
Async XLA Ops:
  1.3 0.9 %copy-start = (f32[8,4096]{1,0:T(8,128)S(1)}, f32[8,4096]{1,0:T(8,128)}, u32[]{:S(2)}) copy-start(f32[8,4096]{1,0:T(8,128)} %k_ref.1) | copy-start | bytes 393220
  2.2 0.7 %copy-start.1 = (s32[6,8]{1,0:T(8,128)S(1)}, s32[6,8]{1,0:T(8,128)}, u32[]{:S(2)}) copy-start(s32[6,8]{1,0:T(8,128)} %nb_ref.1) | copy-start | bytes 580
